TPU v7x, 256 devices: a whole 4x4x8 slice. The times are simulated.
256 devices in a mesh: src: 8 (over y, core), tgt: 32 (over x, z).
Axes of the slice: x: 4, y: 4, z: 8, core: 2. Of those that a mesh axis runs over, the one named last changes fastest.
Arguments:
- source: bfloat16 [16384, 128], P('src'), may hold values from -6 to 6
- target: bfloat16 [32768, 128], P('tgt'), may hold values from -5 to 5
- start_map: float32 [128, 128], replicated, may hold values from -1 to 1
- warm_potential: float32 [32768], P('tgt'), may hold values from -60 to 24
Outputs:
- row_potential: float32 [16384], P('src')
- col_potential: float32 [32768], P('tgt')
- new_map: float32 [128, 128], replicated
All inputs are finite; a program needn't handle non-finite values.
Results may differ from a plain program's by a relative error of at most 0.0078.
Values sent between devices are 32-bit elements; how exact they have to be, the bound alone decides.
A program may use at most 64 MiB of HBM per device.

v0:
```python
import math
import jax
import jax.numpy as jnp
from jax import lax
from jax.sharding import PartitionSpec as P

ROUNDS = 3
NEWTON = 10
EPS = 0.05


def row_partials(rotated, target, col_pot, score_scale):
    row_count = rotated.shape[0]
    block_rows = math.gcd(row_count, 512)
    blocks = rotated.reshape(row_count // block_rows, block_rows, rotated.shape[1])

    def row_one_block(row_block):
        scores = (
            jnp.einsum("rd,cd->rc", row_block, target, preferred_element_type=jnp.float32)
            * score_scale
            + col_pot[None, :]
        )
        peak_val = jnp.max(scores, axis=1)
        totals = jnp.sum(jnp.exp(scores - peak_val[:, None]), axis=1)
        return (peak_val, totals)

    peak_val, totals = lax.map(row_one_block, blocks)
    return (peak_val.reshape(row_count), totals.reshape(row_count))


def col_partials(rotated, target, row_pot, score_scale):
    row_count = rotated.shape[0]
    block_rows = math.gcd(row_count, 512)
    blocks = rotated.reshape(row_count // block_rows, block_rows, rotated.shape[1])
    pots = row_pot.reshape(row_count // block_rows, block_rows)

    def col_one_block(inputs):
        row_block, pot_block = inputs
        scores = (
            jnp.einsum("rd,cd->rc", row_block, target, preferred_element_type=jnp.float32)
            * score_scale
            + pot_block[:, None]
        )
        peak_val = jnp.max(scores, axis=0)
        totals = jnp.sum(jnp.exp(scores - peak_val[None, :]), axis=0)
        return (peak_val, totals)

    peaks, totals = lax.map(col_one_block, (blocks, pots))
    peak_val = jnp.max(peaks, axis=0)
    return (peak_val, jnp.sum(totals * jnp.exp(peaks - peak_val[None, :]), axis=0))


def across_targets(peak_val, totals):
    global_peak = lax.pmax(peak_val, "tgt")
    totals = lax.psum(totals * jnp.exp(peak_val - global_peak), "tgt")
    peak_val = global_peak
    return peak_val + jnp.log(totals)


def across_sources(peak_val, totals):
    global_peak = lax.pmax(peak_val, "src")
    totals = lax.psum(totals * jnp.exp(peak_val - global_peak), "src")
    peak_val = global_peak
    return peak_val + jnp.log(totals)


def polar(matrix):
    iterate = matrix / jnp.sqrt(jnp.sum(matrix * matrix) + 1e-06)
    for newton_index in range(NEWTON):
        gram_matrix = jnp.dot(iterate.T, iterate, precision=lax.Precision.HIGHEST)
        iterate = 1.5 * iterate - 0.5 * jnp.dot(
            iterate, gram_matrix, precision=lax.Precision.HIGHEST
        )
    return iterate


def shards(source, target, start_map, warm_potential):
    width = source.shape[1]
    score_scale = 1.0 / (math.sqrt(width) * EPS)
    rows_all = source.shape[0] * lax.axis_size("src")
    cols_all = target.shape[0] * lax.axis_size("tgt")
    rotated = jnp.dot(
        source, start_map.astype(jnp.bfloat16), preferred_element_type=jnp.float32
    ).astype(jnp.bfloat16)
    col_pot = warm_potential
    for round_index in range(ROUNDS):
        row_pot = -math.log(rows_all) - across_targets(
            *row_partials(rotated, target, col_pot, score_scale)
        )
        col_pot = -math.log(cols_all) - across_sources(
            *col_partials(rotated, target, row_pot, score_scale)
        )
    row_lse = across_targets(*row_partials(rotated, target, col_pot, score_scale))
    row_pot = -math.log(rows_all) - row_lse
    rows_here = source.shape[0] // lax.axis_size("tgt")
    block_rows = math.gcd(rows_here * lax.axis_size("tgt"), 512)
    nblocks = rows_here * lax.axis_size("tgt") // block_rows

    def numerator_one_block(inputs):
        row_block, lse_block = inputs
        scores = (
            jnp.einsum("rd,cd->rc", row_block, target, preferred_element_type=jnp.float32)
            * score_scale
            + col_pot[None, :]
            - lse_block[:, None]
        )
        weights = jnp.exp(scores).astype(jnp.bfloat16)
        return jnp.dot(weights, target, preferred_element_type=jnp.float32)

    parts_out = lax.map(
        numerator_one_block,
        (rotated.reshape(nblocks, block_rows, width), row_lse.reshape(nblocks, block_rows)),
    )
    my_targets = lax.psum_scatter(
        parts_out.reshape(rows_here * lax.axis_size("tgt"), width),
        "tgt",
        scatter_dimension=0,
        tiled=True,
    )
    source_rows = lax.dynamic_slice_in_dim(source, lax.axis_index("tgt") * rows_here, rows_here, 0)
    partial_value = jnp.einsum(
        "rd,re->de", source_rows.astype(jnp.float32), my_targets, precision=lax.Precision.HIGHEST
    )
    covariance_sum = lax.psum(partial_value, ("src", "tgt"))
    new_map = polar(covariance_sum)
    return (EPS * row_pot, EPS * col_pot, new_map)


def solution(mesh):
    placed = (P("src", None), P("tgt", None), P(), P("tgt"))
    return jax.shard_map(
        shards, mesh=mesh, in_specs=placed, out_specs=(P("src"), P("tgt"), P()), check_vma=False
    )
```

profile of v0, /device:TPU:1, one launch (start us, length us, event | category | flops | bytes accessed | tf_op | source)
XLA Modules:
  0.0 1202.2 jit_solution(3626454813866031106)
XLA Ops:
  9.4 8.7 while.94
  18.1 65.3 %pmax.49 = f32[2048]{0:T(1024)S(1)} all-reduce(f32[2048]{0:T(1024)S(1)} %bitcast.221), channel_id=1, replica_groups=mesh['src'=8,'tgt'=32] {'tgt'}, use_global_device_ids=true, to_apply=%region_4.5 | all-reduce | flops 2048 | bytes 16384 | tf_op jit(solution)/shard_map/pmax | solution.py:54
  83.4 56.8 %psum.56 = f32[2048]{0:T(1024)S(1)} all-reduce(f32[2048]{0:T(1024)S(1)} %exponential_multiply_fusion.3), channel_id=1, replica_groups=mesh['src'=8,'tgt'=32] {'tgt'}, use_global_device_ids=true, to_apply=%region_5.6 | all-reduce | flops 2048 | bytes 16384 | tf_op jit(solution)/shard_map/psum | solution.py:55
  140.3 8.4 while.95
  148.7 40.6 %pmax.50 = f32[1024]{0:T(1024)S(1)} all-reduce(f32[1024]{0:T(1024)S(1)} %reduce_max.90), channel_id=1, replica_groups=mesh['src'=8,'tgt'=32] {'src'}, use_global_device_ids=true, to_apply=%region_11.12 | all-reduce | flops 1024 | bytes 8192 | tf_op jit(solution)/shard_map/pmax | solution.py:61
  189.4 12.3 %psum.57 = f32[1024]{0:T(1024)S(1)} all-reduce(f32[1024]{0:T(1024)S(1)} %exponential_multiply_fusion.6), channel_id=1, replica_groups=mesh['src'=8,'tgt'=32] {'src'}, use_global_device_ids=true, to_apply=%region_13.14 | all-reduce | flops 1024 | bytes 8192 | tf_op jit(solution)/shard_map/psum | solution.py:62
  201.7 8.7 while.96
  210.4 58.5 %pmax.51 = f32[2048]{0:T(1024)S(1)} all-reduce(f32[2048]{0:T(1024)S(1)} %bitcast.223), channel_id=1, replica_groups=mesh['src'=8,'tgt'=32] {'tgt'}, use_global_device_ids=true, to_apply=%region_18.19 | all-reduce | flops 2048 | bytes 16384 | tf_op jit(solution)/shard_map/pmax | solution.py:54
  268.9 56.8 %psum.58 = f32[2048]{0:T(1024)S(1)} all-reduce(f32[2048]{0:T(1024)S(1)} %exponential_multiply_fusion.2), channel_id=1, replica_groups=mesh['src'=8,'tgt'=32] {'tgt'}, use_global_device_ids=true, to_apply=%region_19.20 | all-reduce | flops 2048 | bytes 16384 | tf_op jit(solution)/shard_map/psum | solution.py:55
  325.8 8.4 while.97
  334.2 40.5 %pmax.52 = f32[1024]{0:T(1024)S(1)} all-reduce(f32[1024]{0:T(1024)S(1)} %reduce_max.91), channel_id=1, replica_groups=mesh['src'=8,'tgt'=32] {'src'}, use_global_device_ids=true, to_apply=%region_25.26 | all-reduce | flops 1024 | bytes 8192 | tf_op jit(solution)/shard_map/pmax | solution.py:61
  374.8 12.4 %psum.59 = f32[1024]{0:T(1024)S(1)} all-reduce(f32[1024]{0:T(1024)S(1)} %exponential_multiply_fusion.5), channel_id=1, replica_groups=mesh['src'=8,'tgt'=32] {'src'}, use_global_device_ids=true, to_apply=%region_27.28 | all-reduce | flops 1024 | bytes 8192 | tf_op jit(solution)/shard_map/psum | solution.py:62
  387.2 8.7 while.98
  395.9 59.2 %pmax.53 = f32[2048]{0:T(1024)S(1)} all-reduce(f32[2048]{0:T(1024)S(1)} %bitcast.225), channel_id=1, replica_groups=mesh['src'=8,'tgt'=32] {'tgt'}, use_global_device_ids=true, to_apply=%region_32.33 | all-reduce | flops 2048 | bytes 16384 | tf_op jit(solution)/shard_map/pmax | solution.py:54
  455.1 57.0 %psum.60 = f32[2048]{0:T(1024)S(1)} all-reduce(f32[2048]{0:T(1024)S(1)} %exponential_multiply_fusion.1), channel_id=1, replica_groups=mesh['src'=8,'tgt'=32] {'tgt'}, use_global_device_ids=true, to_apply=%region_33.34 | all-reduce | flops 2048 | bytes 16384 | tf_op jit(solution)/shard_map/psum | solution.py:55
  512.2 8.4 while.99
  520.6 39.6 %pmax.54 = f32[1024]{0:T(1024)S(1)} all-reduce(f32[1024]{0:T(1024)S(1)} %reduce_max.92), channel_id=1, replica_groups=mesh['src'=8,'tgt'=32] {'src'}, use_global_device_ids=true, to_apply=%region_39.40 | all-reduce | flops 1024 | bytes 8192 | tf_op jit(solution)/shard_map/pmax | solution.py:61
  560.3 12.4 %psum.61 = f32[1024]{0:T(1024)S(1)} all-reduce(f32[1024]{0:T(1024)S(1)} %exponential_multiply_fusion.4), channel_id=1, replica_groups=mesh['src'=8,'tgt'=32] {'src'}, use_global_device_ids=true, to_apply=%region_41.42 | all-reduce | flops 1024 | bytes 8192 | tf_op jit(solution)/shard_map/psum | solution.py:62
  573.3 8.7 while.100
  582.1 59.2 %pmax.55 = f32[2048]{0:T(1024)S(1)} all-reduce(f32[2048]{0:T(1024)S(1)} %bitcast.227), channel_id=1, replica_groups=mesh['src'=8,'tgt'=32] {'tgt'}, use_global_device_ids=true, to_apply=%region_46.47 | all-reduce | flops 2048 | bytes 16384 | tf_op jit(solution)/shard_map/pmax | solution.py:54
  641.3 57.0 %psum.62 = f32[2048]{0:T(1024)S(1)} all-reduce(f32[2048]{0:T(1024)S(1)} %exponential_multiply_fusion), channel_id=1, replica_groups=mesh['src'=8,'tgt'=32] {'tgt'}, use_global_device_ids=true, to_apply=%region_47.48 | all-reduce | flops 2048 | bytes 16384 | tf_op jit(solution)/shard_map/psum | solution.py:55
  698.9 10.4 while.101
  709.6 228.3 %reduce-scatter.2.cloned.1.call-done = f32[64,128]{1,0:T(8,128)} async-done(((f32[2048,128]{1,0:T(8,128)}), f32[64,128]{1,0:T(8,128)}) %reduce-scatter.2.cloned.1.call-update) | async-done | bytes 32784 | tf_op jit(solution)/shard_map/reduce_scatter | solution.py:114
  939.5 246.2 %all-reduce.2.cloned.1.call-done = f32[128,128]{1,0:T(8,128)} async-done(((f32[128,128]{1,0:T(8,128)}), f32[128,128]{1,0:T(8,128)}) %all-reduce.2.cloned.1.call-update) | async-done | bytes 65552 | tf_op jit(solution)/shard_map/psum | solution.py:124
  (216 shorter events, 83.7 us)
Async XLA Ops:
  7.2 1.0 copy-start
  7.2 930.7 %reduce-scatter.2.cloned.1.call-start = ((), (), s32[]{:S(2)}) async-start(), calls=%async_computation.1 | async-start | bytes 1081344 | tf_op jit(solution)/shard_map/reduce_scatter | solution.py:114
  9.4 1.5 copy-start.1
  11.6 1.5 copy-start.1
  13.7 1.5 copy-start.1
  15.9 1.5 copy-start.1
  709.4 476.4 %all-reduce.2.cloned.1.call-start = ((), (), s32[]{:S(2)}) async-start(), calls=%async_computation.2 | async-start | bytes 131072 | tf_op jit(solution)/shard_map/psum | solution.py:124
Sparse Core Ops, SparseCore 0:
  709.5 228.3 reduce-scatter.1
  944.0 241.7 all-reduce.1
where the time goes:
time: 1200 us
  blocking collectives  628 us (52%)
  waiting for transfers between devices  475 us (40%)
  matrix products  60.8 us (5%)
  other arithmetic  18 us (2%)
  between operations  15.3 us (1%)
    psum x1, waiting for transfers between devices, shards(): covariance_sum = lax.psum(partial_value, ('src', 'tgt'))  246 us
    pmax x4, blocking collectives, across_targets(): global_peak = lax.pmax(peak_val, 'tgt')  242 us
    reduce_scatter x1, waiting for transfers between devices, shards(): lax.psum_scatter(parts_out.reshape(rows_here * lax.axis_size('tgt'), widt...  228 us
    psum x4, blocking collectives, across_targets(): totals = lax.psum(totals * jnp.exp(peak_val - global_peak), 'tgt')  228 us
    pmax x3, blocking collectives, across_sources(): global_peak = lax.pmax(peak_val, 'src')  121 us
    psum x3, blocking collectives, across_sources(): totals = lax.psum(totals * jnp.exp(peak_val - global_peak), 'src')  37.1 us
  transfers between devices with their start and end apart: 2, of which 2 were waited for; matrix products, arithmetic and copies ran while one was open for 0% of the time, Pallas kernels for 0%

commit v1 on v0

--- a/solution.py
+++ b/solution.py
@@ -121,7 +121,7 @@
     partial_value = jnp.einsum(
         "rd,re->de", source_rows.astype(jnp.float32), my_targets, precision=lax.Precision.HIGHEST
     )
-    covariance_sum = lax.psum(partial_value, ("src", "tgt"))
+    covariance_sum = lax.psum(lax.psum(partial_value, "src"), "tgt")
     new_map = polar(covariance_sum)
     return (EPS * row_pot, EPS * col_pot, new_map)
 

time: 1200 us -> 1170 us (0.975)
  waiting for transfers between devices: 475 us -> 435 us
    psum x1 -> x2, waiting for transfers between devices: 246 us -> 207 us  [shards(): covariance_sum = lax.psum(lax.psum(partial_value, 'src'), 'tgt')]
  transfers between devices with their start and end apart: 2 -> 3, of which waited for: 2 -> 3; matrix products, arithmetic and copies ran while one was open for 0% -> 0% of each run, Pallas kernels for 0% -> 0%
where the time goes in v1:
time: 1170 us; the launch traced here: 1160 us
  blocking collectives  628 us (54%)
  waiting for transfers between devices  435 us (37%)
  matrix products  60.8 us (5%)
  other arithmetic  18 us (2%)
  between operations  15 us (1%)
    pmax x4, blocking collectives, across_targets(): global_peak = lax.pmax(peak_val, 'tgt')  242 us
    reduce_scatter x1, waiting for transfers between devices, shards(): lax.psum_scatter(parts_out.reshape(rows_here * lax.axis_size('tgt'), widt...  228 us
    psum x4, blocking collectives, across_targets(): totals = lax.psum(totals * jnp.exp(peak_val - global_peak), 'tgt')  228 us
    psum x2, waiting for transfers between devices, shards(): covariance_sum = lax.psum(lax.psum(partial_value, 'src'), 'tgt')  207 us
    pmax x3, blocking collectives, across_sources(): global_peak = lax.pmax(peak_val, 'src')  121 us
    psum x3, blocking collectives, across_sources(): totals = lax.psum(totals * jnp.exp(peak_val - global_peak), 'src')  37.1 us
    dot_general x16, matrix products, row_one_block(): jnp.einsum('rd,cd->rc', row_block, target, preferred_element_type=jnp.flo...  23.5 us
  transfers between devices with their start and end apart: 3, of which 3 were waited for; matrix products, arithmetic and copies ran while one was open for 0% of the time, Pallas kernels for 0%

profile of v1, /device:TPU:1, one launch (start us, length us, event | category | flops | bytes accessed | tf_op | source)
XLA Modules:
  0.0 1162.5 jit_solution(13095604612107244730)
XLA Ops:
  9.4 8.7 while.94
  18.1 65.3 %pmax.49 = f32[2048]{0:T(1024)S(1)} all-reduce(f32[2048]{0:T(1024)S(1)} %bitcast.221), channel_id=1, replica_groups=mesh['src'=8,'tgt'=32] {'tgt'}, use_global_device_ids=true, to_apply=%region_4.5 | all-reduce | flops 2048 | bytes 16384 | tf_op jit(solution)/shard_map/pmax | solution.py:54
  83.4 56.8 %psum.63 = f32[2048]{0:T(1024)S(1)} all-reduce(f32[2048]{0:T(1024)S(1)} %exponential_multiply_fusion.3), channel_id=1, replica_groups=mesh['src'=8,'tgt'=32] {'tgt'}, use_global_device_ids=true, to_apply=%region_5.6 | all-reduce | flops 2048 | bytes 16384 | tf_op jit(solution)/shard_map/psum | solution.py:55
  140.3 8.4 while.95
  148.7 40.6 %pmax.50 = f32[1024]{0:T(1024)S(1)} all-reduce(f32[1024]{0:T(1024)S(1)} %reduce_max.90), channel_id=1, replica_groups=mesh['src'=8,'tgt'=32] {'src'}, use_global_device_ids=true, to_apply=%region_11.12 | all-reduce | flops 1024 | bytes 8192 | tf_op jit(solution)/shard_map/pmax | solution.py:61
  189.4 12.3 %psum.64 = f32[1024]{0:T(1024)S(1)} all-reduce(f32[1024]{0:T(1024)S(1)} %exponential_multiply_fusion.6), channel_id=1, replica_groups=mesh['src'=8,'tgt'=32] {'src'}, use_global_device_ids=true, to_apply=%region_13.14 | all-reduce | flops 1024 | bytes 8192 | tf_op jit(solution)/shard_map/psum | solution.py:62
  201.7 8.7 while.96
  210.4 58.5 %pmax.51 = f32[2048]{0:T(1024)S(1)} all-reduce(f32[2048]{0:T(1024)S(1)} %bitcast.223), channel_id=1, replica_groups=mesh['src'=8,'tgt'=32] {'tgt'}, use_global_device_ids=true, to_apply=%region_18.19 | all-reduce | flops 2048 | bytes 16384 | tf_op jit(solution)/shard_map/pmax | solution.py:54
  268.9 56.8 %psum.65 = f32[2048]{0:T(1024)S(1)} all-reduce(f32[2048]{0:T(1024)S(1)} %exponential_multiply_fusion.2), channel_id=1, replica_groups=mesh['src'=8,'tgt'=32] {'tgt'}, use_global_device_ids=true, to_apply=%region_19.20 | all-reduce | flops 2048 | bytes 16384 | tf_op jit(solution)/shard_map/psum | solution.py:55
  325.8 8.4 while.97
  334.2 40.5 %pmax.52 = f32[1024]{0:T(1024)S(1)} all-reduce(f32[1024]{0:T(1024)S(1)} %reduce_max.91), channel_id=1, replica_groups=mesh['src'=8,'tgt'=32] {'src'}, use_global_device_ids=true, to_apply=%region_25.26 | all-reduce | flops 1024 | bytes 8192 | tf_op jit(solution)/shard_map/pmax | solution.py:61
  374.8 12.4 %psum.66 = f32[1024]{0:T(1024)S(1)} all-reduce(f32[1024]{0:T(1024)S(1)} %exponential_multiply_fusion.5), channel_id=1, replica_groups=mesh['src'=8,'tgt'=32] {'src'}, use_global_device_ids=true, to_apply=%region_27.28 | all-reduce | flops 1024 | bytes 8192 | tf_op jit(solution)/shard_map/psum | solution.py:62
  387.2 8.7 while.98
  395.9 59.2 %pmax.53 = f32[2048]{0:T(1024)S(1)} all-reduce(f32[2048]{0:T(1024)S(1)} %bitcast.225), channel_id=1, replica_groups=mesh['src'=8,'tgt'=32] {'tgt'}, use_global_device_ids=true, to_apply=%region_32.33 | all-reduce | flops 2048 | bytes 16384 | tf_op jit(solution)/shard_map/pmax | solution.py:54
  455.1 57.0 %psum.67 = f32[2048]{0:T(1024)S(1)} all-reduce(f32[2048]{0:T(1024)S(1)} %exponential_multiply_fusion.1), channel_id=1, replica_groups=mesh['src'=8,'tgt'=32] {'tgt'}, use_global_device_ids=true, to_apply=%region_33.34 | all-reduce | flops 2048 | bytes 16384 | tf_op jit(solution)/shard_map/psum | solution.py:55
  520.6 39.6 %pmax.54 = f32[1024]{0:T(1024)S(1)} all-reduce(f32[1024]{0:T(1024)S(1)} %reduce_max.92), channel_id=1, replica_groups=mesh['src'=8,'tgt'=32] {'src'}, use_global_device_ids=true, to_apply=%region_39.40 | all-reduce | flops 1024 | bytes 8192 | tf_op jit(solution)/shard_map/pmax | solution.py:61
  560.3 12.4 %psum.68 = f32[1024]{0:T(1024)S(1)} all-reduce(f32[1024]{0:T(1024)S(1)} %exponential_multiply_fusion.4), channel_id=1, replica_groups=mesh['src'=8,'tgt'=32] {'src'}, use_global_device_ids=true, to_apply=%region_41.42 | all-reduce | flops 1024 | bytes 8192 | tf_op jit(solution)/shard_map/psum | solution.py:62
  573.3 8.7 while.100
  582.1 59.2 %pmax.55 = f32[2048]{0:T(1024)S(1)} all-reduce(f32[2048]{0:T(1024)S(1)} %bitcast.227), channel_id=1, replica_groups=mesh['src'=8,'tgt'=32] {'tgt'}, use_global_device_ids=true, to_apply=%region_46.47 | all-reduce | flops 2048 | bytes 16384 | tf_op jit(solution)/shard_map/pmax | solution.py:54
  641.3 57.0 %psum.69 = f32[2048]{0:T(1024)S(1)} all-reduce(f32[2048]{0:T(1024)S(1)} %exponential_multiply_fusion), channel_id=1, replica_groups=mesh['src'=8,'tgt'=32] {'tgt'}, use_global_device_ids=true, to_apply=%region_47.48 | all-reduce | flops 2048 | bytes 16384 | tf_op jit(solution)/shard_map/psum | solution.py:55
  698.9 10.4 while.101
  709.4 228.5 %reduce-scatter.2.cloned.1.call-done = f32[64,128]{1,0:T(8,128)} async-done(((f32[2048,128]{1,0:T(8,128)}), f32[64,128]{1,0:T(8,128)}) %reduce-scatter.2.cloned.1.call-update) | async-done | bytes 32784 | tf_op jit(solution)/shard_map/reduce_scatter | solution.py:114
  939.8 66.6 %all-reduce.3.cloned.1.call-done = f32[128,128]{1,0:T(8,128)} async-done(((f32[128,128]{1,0:T(8,128)}), f32[128,128]{1,0:T(8,128)}) %all-reduce.3.cloned.1.call-update) | async-done | bytes 65552 | tf_op jit(solution)/shard_map/psum | solution.py:124
  1006.4 139.9 %all-reduce.5.cloned.1.call-done = f32[128,128]{1,0:T(8,128)} async-done(((f32[128,128]{1,0:T(8,128)}), f32[128,128]{1,0:T(8,128)}) %all-reduce.5.cloned.1.call-update) | async-done | bytes 65552 | tf_op jit(solution)/shard_map/psum | solution.py:124
  (219 shorter events, 92.1 us)
Async XLA Ops:
  7.2 1.0 copy-start
  7.2 930.7 %reduce-scatter.2.cloned.1.call-start = ((), (), s32[]{:S(2)}) async-start(), calls=%async_computation.1 | async-start | bytes 1081344 | tf_op jit(solution)/shard_map/reduce_scatter | solution.py:114
  9.4 1.5 copy-start.1
  11.6 1.5 copy-start.1
  13.7 1.5 copy-start.1
  15.9 1.5 copy-start.1
  709.4 297.0 %all-reduce.3.cloned.1.call-start = ((), (), s32[]{:S(2)}) async-start(), calls=%async_computation.2 | async-start | bytes 131072 | tf_op jit(solution)/shard_map/psum | solution.py:124
  939.5 206.8 %all-reduce.5.cloned.1.call-start = ((), (), s32[]{:S(2)}) async-start(), calls=%async_computation.3 | async-start | bytes 131072 | tf_op jit(solution)/shard_map/psum | solution.py:124
Sparse Core Ops, SparseCore 0:
  709.5 228.3 reduce-scatter.1
  940.8 65.5 all-reduce.2
  1010.2 136.0 all-reduce.4
